TPU v7x, 32 devices: a whole 2x2x4 slice. The times are simulated.
32 devices in a mesh: seq: 4 (over x, core), shard: 8 (over z, y).
Axes of the slice: x: 2, y: 2, z: 4, core: 2. Of those that a mesh axis runs over, the one named last changes fastest.
Arguments:
- tokens: bfloat16 [8, 2048, 1024], P('shard', 'seq'), may hold values from -6 to 6
- cotangent: bfloat16 [8, 2048, 1024], P('shard', 'seq'), may hold values from -6 to 6
- entry_weight: float32 [1024, 3072], P(('seq', 'shard')), may hold values from -0.1875 to 0.1875
- entry_drift: float32 [1024, 3072], P(('seq', 'shard')), may hold values from -64 to 64
- entry_power: float32 [1024, 3072], P(('seq', 'shard')), may hold values from 8.192 to 32.768
- exit_weight: float32 [1024, 1024], P(('seq', 'shard')), may hold values from -6 to 6
- exit_drift: float32 [1024, 1024], P(('seq', 'shard')), may hold values from -4 to 4
- exit_power: float32 [1024, 1024], P(('seq', 'shard')), may hold values from 0.0064 to 0.0256
- expand_weight: float32 [1024, 4096], P(('seq', 'shard')), may hold values from -0.1875 to 0.1875
- expand_drift: float32 [1024, 4096], P(('seq', 'shard')), may hold values from -16 to 16
- expand_power: float32 [1024, 4096], P(('seq', 'shard')), may hold values from 0.65536 to 2.62144
- reduce_weight: float32 [4096, 1024], P(('seq', 'shard')), may hold values from -0.09375 to 0.09375
- reduce_drift: float32 [4096, 1024], P(('seq', 'shard')), may hold values from -40 to 40
- reduce_power: float32 [4096, 1024], P(('seq', 'shard')), may hold values from 3.2768 to 13.1072
- vectors: float32 [12, 1024], P(None, ('seq', 'shard')), may hold values from -1 to 1.3, as said below
- vectors_drift: float32 [12, 1024], P(None, ('seq', 'shard')), may hold values from -71.04 to 71.04, as said below
- vectors_power: float32 [12, 1024], P(None, ('seq', 'shard')), may hold values from 0.65536 to 65.536, as said below
Outputs:
- block_out: bfloat16 [8, 2048, 1024], P('shard', 'seq')
- input_grad: float32 [8, 2048, 1024], P('shard', 'seq')
- drift_entry: float32 [1024, 3072], P(('seq', 'shard'))
- power_entry: float32 [1024, 3072], P(('seq', 'shard'))
- moved_entry: float32 [1024, 3072], P(('seq', 'shard'))
- drift_exit: float32 [1024, 1024], P(('seq', 'shard'))
- power_exit: float32 [1024, 1024], P(('seq', 'shard'))
- moved_exit: float32 [1024, 1024], P(('seq', 'shard'))
- drift_expand: float32 [1024, 4096], P(('seq', 'shard'))
- power_expand: float32 [1024, 4096], P(('seq', 'shard'))
- moved_expand: float32 [1024, 4096], P(('seq', 'shard'))
- drift_reduce: float32 [4096, 1024], P(('seq', 'shard'))
- power_reduce: float32 [4096, 1024], P(('seq', 'shard'))
- moved_reduce: float32 [4096, 1024], P(('seq', 'shard'))
- drift_vectors: float32 [12, 1024], P(None, ('seq', 'shard'))
- power_vectors: float32 [12, 1024], P(None, ('seq', 'shard'))
- moved_vectors: float32 [12, 1024], P(None, ('seq', 'shard'))
Inputs may be any that keep to these rules, and one draw needn't show every extreme that they name: `vectors`: rows 3 and 6 are gains near one, the others biases. `vectors_drift`: both signs. `vectors_power`: positive.
All inputs are finite; a program needn't handle non-finite values.
Results may differ from a plain program's by a relative error of at most 0.012.
The roundings to bfloat16 on the way count: a program that leaves them out, or rounds other values in their place, can miss the bound.
Values may be sent and summed in bfloat16 or wider, within the bound.
A program may use at most 192 MiB of HBM per device.

v0:
```python
import jax
import jax.numpy as jnp
from jax import lax
from jax.sharding import PartitionSpec as P

HEAD_DIM = 64
QBLK = 512
STEP = 10


NORM_EPS = 1e-05
ADAM_EPS = 1e-06
DECAY_ONE = 0.9
DECAY_TWO = 0.999


def exact_gelu(inside):
    return jax.nn.gelu(inside, approximate=False)


def norm_forward(summed, gain_row, shift_row):
    centre = jnp.mean(summed, axis=-1, keepdims=True)
    centred = summed - centre
    inverse = lax.rsqrt(jnp.mean(centred * centred, axis=-1, keepdims=True) + NORM_EPS)
    normed = centred * inverse
    return (normed * gain_row + shift_row, normed, inverse)


def norm_backward(upstream, normed, inverse, gain_row):
    gain_grad = jnp.sum(upstream * normed, axis=0)
    shift_grad = jnp.sum(upstream, axis=0)
    scaled = upstream * gain_row
    bracket = (
        scaled
        - jnp.mean(scaled, axis=-1, keepdims=True)
        - normed * jnp.mean(scaled * normed, axis=-1, keepdims=True)
    )
    return (inverse * bracket, gain_grad, shift_grad)


def by_blocks(tensor):
    seq_count, length = (tensor.shape[0], tensor.shape[1])
    shaped = tensor.reshape((seq_count, length // QBLK, QBLK) + tensor.shape[2:])
    return jnp.moveaxis(shaped, 1, 0)


def from_blocks(tensor):
    swapped = jnp.moveaxis(tensor, 0, 1)
    return swapped.reshape(
        (swapped.shape[0], swapped.shape[1] * swapped.shape[2]) + swapped.shape[3:]
    )


def attend_forward(queries, key_rows, value_rows):

    def one_block(query_block):
        scores = (
            jnp.einsum("sqhd,skhd->shqk", query_block, key_rows, preferred_element_type=jnp.float32)
            * 0.125
        )
        highest = jnp.max(scores, axis=-1, keepdims=True)
        summed = jnp.sum(jnp.exp(scores - highest), axis=-1, keepdims=True)
        log_total = highest + jnp.log(summed)
        weights = jnp.exp(scores - log_total).astype(jnp.bfloat16)
        context = jnp.einsum(
            "shqk,skhd->sqhd", weights, value_rows, preferred_element_type=jnp.float32
        )
        return (context.astype(jnp.bfloat16), log_total[..., 0])

    context, log_total = lax.map(one_block, by_blocks(queries))
    return (from_blocks(context), log_total)


def attend_backward(queries, key_rows, value_rows, log_total, upstream):

    def one_block(totals, inputs):
        key_grad, value_grad = totals
        query_block, upstream_block, log_block = inputs
        scores = (
            jnp.einsum("sqhd,skhd->shqk", query_block, key_rows, preferred_element_type=jnp.float32)
            * 0.125
        )
        weights = jnp.exp(scores - log_block[..., None])
        weight_grad = jnp.einsum(
            "sqhd,skhd->shqk", upstream_block, value_rows, preferred_element_type=jnp.float32
        )
        centre = jnp.sum(weights * weight_grad, axis=-1, keepdims=True)
        score_grad = (weights * (weight_grad - centre)).astype(jnp.bfloat16)
        query_grad = (
            jnp.einsum("shqk,skhd->sqhd", score_grad, key_rows, preferred_element_type=jnp.float32)
            * 0.125
        )
        key_grad = (
            key_grad
            + jnp.einsum(
                "shqk,sqhd->skhd", score_grad, query_block, preferred_element_type=jnp.float32
            )
            * 0.125
        )
        value_grad = value_grad + jnp.einsum(
            "shqk,sqhd->skhd",
            weights.astype(jnp.bfloat16),
            upstream_block,
            preferred_element_type=jnp.float32,
        )
        return ((key_grad, value_grad), query_grad)

    empty_grad = jnp.zeros(key_rows.shape, jnp.float32)
    totals, query_grad = lax.scan(
        one_block, (empty_grad, empty_grad), (by_blocks(queries), by_blocks(upstream), log_total)
    )
    return (from_blocks(query_grad), totals[0], totals[1])


def adam_step(weight, drift_old, power_old, gradient, step_rate, decay_rate):
    drift_new = DECAY_ONE * drift_old + (1.0 - DECAY_ONE) * gradient
    power_new = DECAY_TWO * power_old + (1.0 - DECAY_TWO) * gradient * gradient
    normalized = (
        drift_new
        / (1.0 - DECAY_ONE**STEP)
        / (jnp.sqrt(power_new / (1.0 - DECAY_TWO**STEP)) + ADAM_EPS)
    )
    return (drift_new, power_new, weight - step_rate * (normalized + decay_rate * weight))


def body(
    tokens,
    cotangent,
    entry_weight,
    entry_drift,
    entry_power,
    exit_weight,
    exit_drift,
    exit_power,
    expand_weight,
    expand_drift,
    expand_power,
    reduce_weight,
    reduce_drift,
    reduce_power,
    vectors,
    vectors_drift,
    vectors_power,
):
    entry_low, exit_low, expand_low, reduce_low, vector_low = (
        lax.all_gather(entry_weight.astype(jnp.bfloat16), ("seq", "shard"), axis=0, tiled=True),
        lax.all_gather(exit_weight.astype(jnp.bfloat16), ("seq", "shard"), axis=0, tiled=True),
        lax.all_gather(expand_weight.astype(jnp.bfloat16), ("seq", "shard"), axis=0, tiled=True),
        lax.all_gather(reduce_weight.astype(jnp.bfloat16), ("seq", "shard"), axis=0, tiled=True),
        lax.all_gather(vectors.astype(jnp.bfloat16), ("seq", "shard"), axis=1, tiled=True),
    )
    vector_rows = vector_low.astype(jnp.float32)
    seq_count, local_len, width = tokens.shape
    row_count = seq_count * local_len
    groups = lax.axis_size("seq")
    slot_width = width // groups
    head_count = slot_width // HEAD_DIM
    inputs = tokens.reshape(row_count, width)

    def to_slots(matrix):
        return matrix.reshape(seq_count, local_len, groups, slot_width)

    def heads_view(tensor):
        return tensor.reshape(seq_count, tensor.shape[1], head_count, HEAD_DIM)

    bias_entry = jnp.concatenate([vector_rows[0], jnp.zeros((width,), jnp.float32), vector_rows[1]])
    projected = (
        jnp.dot(inputs, entry_low, preferred_element_type=jnp.float32) + bias_entry
    ).astype(jnp.bfloat16)
    queries, key_rows, value_rows = (
        lax.all_to_all(
            to_slots(projected[:, :width]), "seq", split_axis=2, concat_axis=1, tiled=True
        ),
        lax.all_to_all(
            to_slots(projected[:, width : 2 * width]),
            "seq",
            split_axis=2,
            concat_axis=1,
            tiled=True,
        ),
        lax.all_to_all(
            to_slots(projected[:, 2 * width :]), "seq", split_axis=2, concat_axis=1, tiled=True
        ),
    )
    queries, key_rows, value_rows = (
        heads_view(queries),
        heads_view(key_rows),
        heads_view(value_rows),
    )
    full_len = queries.shape[1]
    context_heads, log_total = attend_forward(queries, key_rows, value_rows)
    context = lax.all_to_all(
        context_heads.reshape(seq_count, full_len, 1, slot_width),
        "seq",
        split_axis=1,
        concat_axis=2,
        tiled=True,
    ).reshape(row_count, width)
    attended = jnp.dot(context, exit_low, preferred_element_type=jnp.float32) + vector_rows[2]
    first_sum = inputs.astype(jnp.float32) + attended
    mixed_rows, normed_one, inverse_one = norm_forward(first_sum, vector_rows[3], vector_rows[4])
    mixed_low = mixed_rows.astype(jnp.bfloat16)
    pre_act = jnp.dot(mixed_low, expand_low, preferred_element_type=jnp.float32) + vector_rows[
        8:
    ].reshape(-1)
    activated, gelu_pull = jax.vjp(exact_gelu, pre_act)
    act_low = activated.astype(jnp.bfloat16)
    branch = jnp.dot(act_low, reduce_low, preferred_element_type=jnp.float32) + vector_rows[5]
    second_sum = mixed_rows + branch
    result, normed_two, inverse_two = norm_forward(second_sum, vector_rows[6], vector_rows[7])
    block_out = result.astype(jnp.bfloat16).reshape(tokens.shape)
    entry_low, exit_low, expand_low, reduce_low, vector_low = (
        lax.all_gather(entry_weight.astype(jnp.bfloat16), ("seq", "shard"), axis=0, tiled=True),
        lax.all_gather(exit_weight.astype(jnp.bfloat16), ("seq", "shard"), axis=0, tiled=True),
        lax.all_gather(expand_weight.astype(jnp.bfloat16), ("seq", "shard"), axis=0, tiled=True),
        lax.all_gather(reduce_weight.astype(jnp.bfloat16), ("seq", "shard"), axis=0, tiled=True),
        lax.all_gather(vectors.astype(jnp.bfloat16), ("seq", "shard"), axis=1, tiled=True),
    )
    vector_rows = vector_low.astype(jnp.float32)
    upstream = cotangent.reshape(row_count, width).astype(jnp.float32)
    second_grad, gain_two, shift_two = norm_backward(
        upstream, normed_two, inverse_two, vector_rows[6]
    )
    branch_grad = second_grad.astype(jnp.bfloat16)
    reduce_grad = jnp.einsum("rf,rd->fd", act_low, branch_grad, preferred_element_type=jnp.float32)
    branch_bias = jnp.sum(branch_grad.astype(jnp.float32), axis=0)
    act_grad = jnp.einsum("rd,fd->rf", branch_grad, reduce_low, preferred_element_type=jnp.float32)
    pre_grad = gelu_pull(act_grad)[0].astype(jnp.bfloat16)
    expand_grad = jnp.einsum("rd,rf->df", mixed_low, pre_grad, preferred_element_type=jnp.float32)
    expand_bias = jnp.sum(pre_grad.astype(jnp.float32), axis=0).reshape(4, width)
    mixed_grad = second_grad + jnp.einsum(
        "rf,df->rd", pre_grad, expand_low, preferred_element_type=jnp.float32
    )
    vector_back = jnp.concatenate(
        [branch_bias[None], gain_two[None], shift_two[None], expand_bias], axis=0
    )
    first_grad, gain_one, shift_one = norm_backward(
        mixed_grad, normed_one, inverse_one, vector_rows[3]
    )
    attended_grad = first_grad.astype(jnp.bfloat16)
    exit_grad = jnp.einsum("rc,rd->cd", context, attended_grad, preferred_element_type=jnp.float32)
    exit_bias = jnp.sum(attended_grad.astype(jnp.float32), axis=0)
    context_grad = jnp.einsum(
        "rd,cd->rc", attended_grad, exit_low, preferred_element_type=jnp.float32
    ).astype(jnp.bfloat16)
    context_heads_grad = lax.all_to_all(
        to_slots(context_grad), "seq", split_axis=2, concat_axis=1, tiled=True
    )
    query_grad, key_grad, value_grad = attend_backward(
        queries, key_rows, value_rows, log_total, heads_view(context_heads_grad)
    )

    def back_slots(tensor):
        return tensor.astype(jnp.bfloat16).reshape(seq_count, full_len, 1, slot_width)

    query_back, key_back, value_back = (
        lax.all_to_all(back_slots(query_grad), "seq", split_axis=1, concat_axis=2, tiled=True),
        lax.all_to_all(back_slots(key_grad), "seq", split_axis=1, concat_axis=2, tiled=True),
        lax.all_to_all(back_slots(value_grad), "seq", split_axis=1, concat_axis=2, tiled=True),
    )
    entry_back = jnp.concatenate(
        [
            query_back.reshape(row_count, width),
            key_back.reshape(row_count, width),
            value_back.reshape(row_count, width),
        ],
        axis=1,
    )
    entry_grad = jnp.einsum("rd,re->de", inputs, entry_back, preferred_element_type=jnp.float32)
    bias_sums = jnp.sum(entry_back.astype(jnp.float32), axis=0)
    input_grad = first_grad + jnp.einsum(
        "re,de->rd", entry_back, entry_low, preferred_element_type=jnp.float32
    )
    vector_front = jnp.stack(
        [bias_sums[:width], bias_sums[2 * width :], exit_bias, gain_one, shift_one], axis=0
    )
    summed_entry, summed_exit, summed_expand, summed_reduce, summed_vectors = (
        lax.psum_scatter(entry_grad, ("seq", "shard"), scatter_dimension=0, tiled=True),
        lax.psum_scatter(exit_grad, ("seq", "shard"), scatter_dimension=0, tiled=True),
        lax.psum_scatter(expand_grad, ("seq", "shard"), scatter_dimension=0, tiled=True),
        lax.psum_scatter(reduce_grad, ("seq", "shard"), scatter_dimension=0, tiled=True),
        lax.psum_scatter(
            jnp.concatenate([vector_front, vector_back], axis=0),
            ("seq", "shard"),
            scatter_dimension=1,
            tiled=True,
        ),
    )
    entry_new = adam_step(entry_weight, entry_drift, entry_power, summed_entry, 0.03, 0.01)
    exit_new = adam_step(exit_weight, exit_drift, exit_power, summed_exit, 0.3, 0.01)
    expand_new = adam_step(expand_weight, expand_drift, expand_power, summed_expand, 0.03, 0.01)
    reduce_new = adam_step(reduce_weight, reduce_drift, reduce_power, summed_reduce, 0.02, 0.01)
    vectors_new = adam_step(vectors, vectors_drift, vectors_power, summed_vectors, 0.2, 0.0)
    return (
        block_out,
        input_grad.reshape(tokens.shape),
        entry_new[0],
        entry_new[1],
        entry_new[2],
        exit_new[0],
        exit_new[1],
        exit_new[2],
        expand_new[0],
        expand_new[1],
        expand_new[2],
        reduce_new[0],
        reduce_new[1],
        reduce_new[2],
        vectors_new[0],
        vectors_new[1],
        vectors_new[2],
    )


def solution(mesh):
    in_specs = (
        P("shard", "seq", None),
        P("shard", "seq", None),
        P(("seq", "shard"), None),
        P(("seq", "shard"), None),
        P(("seq", "shard"), None),
        P(("seq", "shard"), None),
        P(("seq", "shard"), None),
        P(("seq", "shard"), None),
        P(("seq", "shard"), None),
        P(("seq", "shard"), None),
        P(("seq", "shard"), None),
        P(("seq", "shard"), None),
        P(("seq", "shard"), None),
        P(("seq", "shard"), None),
        P(None, ("seq", "shard")),
        P(None, ("seq", "shard")),
        P(None, ("seq", "shard")),
    )
    out_specs = (
        P("shard", "seq", None),
        P("shard", "seq", None),
        P(("seq", "shard"), None),
        P(("seq", "shard"), None),
        P(("seq", "shard"), None),
        P(("seq", "shard"), None),
        P(("seq", "shard"), None),
        P(("seq", "shard"), None),
        P(("seq", "shard"), None),
        P(("seq", "shard"), None),
        P(("seq", "shard"), None),
        P(("seq", "shard"), None),
        P(("seq", "shard"), None),
        P(("seq", "shard"), None),
        P(None, ("seq", "shard")),
        P(None, ("seq", "shard")),
        P(None, ("seq", "shard")),
    )
    return jax.shard_map(body, mesh=mesh, in_specs=in_specs, out_specs=out_specs, check_vma=False)
```

profile of v0, /device:TPU:0, one launch (start us, length us, event | category | flops | bytes accessed | tf_op | source)
XLA Modules:
  0.0 1831.5 jit_solution(15979284903775134882)
XLA Ops:
  13.1 71.3 %all-gather = bf16[32,32,12]{1,2,0:T(8,128)(2,1)S(1)} all-gather(bf16[1,32,12]{1,2,0:T(8,128)(2,1)S(1)} %convert_bitcast_fusion.1), channel_id=1, replica_groups=mesh['seq'=4,'shard'=8] {'seq','shard'}, dimensions={0}, use_global_device_ids=true | all-gather | bytes 25344 | tf_op jit(solution)/shard_map/all_gather | solution.py:150
  85.2 6.5 add_convert_fusion.1
  100.5 12.5 all-to-all-done.1
  119.5 12.8 all-to-all-done.2
  142.7 8.4 all-to-all-done
  152.6 66.8 %while.27 = (s32[]{:T(128)}, bf16[4,1,512,4,64]{2,4,3,1,0:T(8,128)(2,1)}, f32[4,1,4,512]{3,2,1,0:T(4,128)S(1)}, bf16[4,1,512,4,64]{2,4,3,1,0:T(8,128)(2,1)S(1)},...) while((s32[]{:T(128)}, bf16[4,1,512,4,64]{2,4,3,1,0:T(8,128)(2,1)}, ...), condition=%wide.region_3.4_spmd, body=%wide.region_0.3_spmd.sunk | while | flops 1107425280 | bytes 120128112 | solution.py:70
  160.9 8.1 fusion.124
  177.3 8.2 fusion.124
  194.7 8.2 fusion.124
  211.2 8.2 fusion.124
  223.4 8.2 reshape.283
  232.2 12.6 reduce.7
  252.7 19.3 %all-to-all-done.3 = bf16[4,2,65536]{2,1,0:T(2,128)(2,1)} async-done(((bf16[4,2,65536]{2,1,0:T(2,128)(2,1)}), bf16[4,2,65536]{2,1,0:T(2,128)(2,1)}, u32[]{:S(2)}, u32[]{:S(2)}) %all-to-all-start.3) | async-done | bytes 1048608 | tf_op jit(solution)/shard_map/all_to_all | solution.py:192
  286.3 28.2 %multiply_convert_fusion.1 = (bf16[512,4096]{1,0:T(8,128)(2,1)}, f32[512,4096]{1,0:T(8,128)}, f32[512,4096]{1,0:T(8,128)}) fusion(f32[4096]{0:T(1024)S(1)} %bitcast.286, bf16[1024,4096]{1,0:T(8,128)(2,1)} %all-gather.10.cloned.1.call-done, f32[512,1024]{1,0:T(8,128)} %copy-done.5, f32[1024]{0:T(1024)S(1)} %bitcast.294, f32[1024]{0:T(1024)S(1)} %bitcast.277, ...), kind=kOutput, calls=%fused_computation.54 | convolution fusion | flops 4436000768 | bytes 31485952 | tf_op jit(solution)/shard_map/dot_general | solution.py:203
  314.6 10.0 fusion.92
  328.8 16.1 convert_reduce_fusion
  344.9 10.0 multiply_reduce_fusion.2
  369.2 14.5 all-to-all-done.4
  386.0 176.8 %while.28 = (s32[]{:T(128)}, f32[1,2048,4,64]{1,3,2,0:T(8,128)}, f32[1,2048,4,64]{1,3,2,0:T(8,128)}, bf16[4,1,512,4,64]{2,4,3,1,0:T(8,128)(2,1)}, bf16[4,1,512,4...) while((s32[]{:T(128)}, f32[1,2048,4,64]{1,3,2,0:T(8,128)}, ...), condition=%wide.region_14.15_spmd.clone, body=%wide.region_12.14_spmd.clone.sunk | while | flops 2737436672 | bytes 273213120 | solution.py:109
  388.4 10.1 multiply_reduce_fusion.10
  399.2 10.5 multiply_convert_fusion.3
  416.1 7.5 fusion.136
  431.5 10.1 multiply_reduce_fusion.10
  442.3 10.5 multiply_convert_fusion.3
  452.8 7.1 fusion.134
  459.9 7.5 fusion.136
  476.0 10.1 multiply_reduce_fusion.10
  486.8 10.5 multiply_convert_fusion.3
  497.3 7.1 fusion.134
  504.4 7.5 fusion.136
  520.6 10.1 multiply_reduce_fusion.10
  531.4 10.5 multiply_convert_fusion.3
  541.9 7.1 fusion.134
  548.9 7.5 fusion.136
  566.9 8.5 reshape.284
  575.4 11.6 reduce.10
  596.9 11.6 reduce.9
  620.2 11.6 reduce.8
  670.1 10.2 convolution_bitcast_fusion
  680.3 12.6 copy.192
  694.5 10.5 fusion.77
  706.7 10.7 fusion.71
  719.2 8.3 add_bitcast_fusion
  727.5 72.8 %reduce-scatter.18.cloned.1.call-done = f32[32,12]{1,0:T(8,128)} async-done(((f32[1024,12]{1,0:T(8,128)}), f32[32,12]{1,0:T(8,128)}) %reduce-scatter.18.cloned.1.call-update) | async-done | bytes 1552
  802.4 140.6 %reduce-scatter.10.cloned.1.call-done = f32[32,1024]{1,0:T(8,128)} async-done(((f32[1024,1024]{1,0:T(8,128)}), f32[32,1024]{1,0:T(8,128)}) %reduce-scatter.10.cloned.1.call-update) | async-done | bytes 131088 | tf_op jit(solution)/shard_map/reduce_scatter | solution.py:279
  944.9 158.1 %reduce-scatter.16.cloned.1.call-done = f32[32,3072]{1,0:T(8,128)} async-done(((f32[1024,3072]{1,0:T(8,128)}), f32[32,3072]{1,0:T(8,128)}) %reduce-scatter.16.cloned.1.call-update) | async-done | bytes 393232 | tf_op jit(solution)/shard_map/reduce_scatter | solution.py:278
  1105.5 357.1 %reduce-scatter.12.cloned.1.call-done = f32[32,4096]{1,0:T(8,128)} async-done(((f32[1024,4096]{1,0:T(8,128)}), f32[32,4096]{1,0:T(8,128)}) %reduce-scatter.12.cloned.1.call-update) | async-done | bytes 524304 | tf_op jit(solution)/shard_map/reduce_scatter | solution.py:280
  1465.4 356.8 %reduce-scatter.14.cloned.1.call-done = f32[128,1024]{1,0:T(8,128)} async-done(((f32[4096,1024]{1,0:T(8,128)}), f32[128,1024]{1,0:T(8,128)}) %reduce-scatter.14.cloned.1.call-update) | async-done | bytes 524304 | tf_op jit(solution)/shard_map/reduce_scatter | solution.py:281
  (240 shorter events, 238.9 us)
Async XLA Ops:
  7.2 78.0 %all-gather.6.cloned.1.call-start = ((), (), s32[]{:S(2)}) async-start(), calls=%async_computation.13 | async-start | bytes 6488064 | tf_op jit(solution)/shard_map/all_gather | solution.py:146
  9.0 272.1 %all-gather.8.cloned.1.call-start = ((), (), s32[]{:S(2)}) async-start(), calls=%async_computation.14 | async-start | bytes 2162688 | tf_op jit(solution)/shard_map/all_gather | solution.py:147
  10.6 275.7 %all-gather.10.cloned.1.call-start = ((), (), s32[]{:S(2)}) async-start(), calls=%async_computation.15 | async-start | bytes 8650752 | tf_op jit(solution)/shard_map/all_gather | solution.py:148
  85.2 229.3 %copy-start.36 = (f32[1,1024]{1,0:T(1,128)}, f32[1,1024]{1,0:T(1,128)S(1)}, u32[]{:S(2)}) copy-start(f32[1,1024]{1,0:T(1,128)S(1)} %get-tuple-element.352) | copy-start | bytes 12292
  85.2 269.7 %copy-start.26 = (f32[1,1024]{1,0:T(1,128)}, f32[1,1024]{1,0:T(1,128)S(1)}, u32[]{:S(2)}) copy-start(f32[1,1024]{1,0:T(1,128)S(1)} %get-tuple-element.353) | copy-start | bytes 12292
  95.0 18.0 all-to-all-start.1
  113.0 19.3 %all-to-all-start.2 = ((bf16[1,512,4,256]{3,1,0,2:T(8,128)(2,1)}), bf16[1,512,4,256]{3,1,0,2:T(8,128)(2,1)S(1)}, u32[]{:S(2)}, u32[]{:S(2)}) async-start(bf16[1,512,4,256]{3,1,0,2:T(8,128)(2,1)} %copy.170), calls=%async_computation.2 | async-start | bytes 2097152 | tf_op jit(solution)/shard_map/all_to_all | solution.py:181
  132.3 18.8 %all-to-all-start = ((bf16[1,512,4,256]{3,1,0,2:T(8,128)(2,1)}), bf16[1,512,4,256]{3,1,0,2:T(8,128)(2,1)}, u32[]{:S(2)}, u32[]{:S(2)}) async-start(bf16[1,512,4,256]{3,1,0,2:T(8,128)(2,1)} %copy.166), calls=%async_computation | async-start | bytes 2097152 | tf_op jit(solution)/shard_map/all_to_all | solution.py:171
  136.6 177.9 %all-gather.12.cloned.1.call-start = ((), (), s32[]{:S(2)}) async-start(), calls=%async_computation.16 | async-start | bytes 8650752 | tf_op jit(solution)/shard_map/all_gather | solution.py:149
  248.3 23.8 %all-to-all-start.3 = ((bf16[4,2,65536]{2,1,0:T(2,128)(2,1)}), bf16[4,2,65536]{2,1,0:T(2,128)(2,1)}, u32[]{:S(2)}, u32[]{:S(2)}) async-start(bf16[4,2,65536]{2,1,0:T(2,128)(2,1)} %reshape.289), calls=%async_computation.3 | async-start | bytes 2097152 | tf_op jit(solution)/shard_map/all_to_all | solution.py:192
  284.6 70.3 %copy-start.24 = (f32[512]{0:T(512)}, f32[512]{0:T(512)S(1)}, u32[]{:S(2)}) copy-start(f32[512]{0:T(512)S(1)} %broadcast_multiply_fusion.5) | copy-start | bytes 6148
  286.3 68.7 %copy-start.33 = (f32[512]{0:T(512)}, f32[512]{0:T(512)S(1)}, u32[]{:S(2)}) copy-start(f32[512]{0:T(512)S(1)} %add_rsqrt_fusion.1) | copy-start | bytes 6148
  286.3 28.2 %copy-start.38 = (f32[1,1024]{1,0:T(1,128)S(1)}, f32[1,1024]{1,0:T(1,128)}, u32[]{:S(2)}) copy-start(f32[1,1024]{1,0:T(1,128)} %get-tuple-element.351) | copy-start | bytes 12292
  314.6 11.8 copy-start.31
  328.8 16.1 copy-start.17
  328.8 16.1 copy-start.6
  364.9 18.8 %all-to-all-start.4 = ((bf16[1,512,4,256]{3,1,0,2:T(8,128)(2,1)}), bf16[1,512,4,256]{3,1,0,2:T(8,128)(2,1)}, u32[]{:S(2)}, u32[]{:S(2)}) async-start(bf16[1,512,4,256]{3,1,0,2:T(8,128)(2,1)} %copy.176), calls=%async_computation.4 | async-start | bytes 2097152 | tf_op jit(solution)/shard_map/all_to_all | solution.py:246
  388.3 10.8 copy-start
  409.6 13.9 copy-start.1
  452.8 14.6 copy-start.1
  497.3 14.6 copy-start.1
  520.6 10.8 copy-start
  541.9 14.6 copy-start.1
  566.9 26.1 %copy-start.3 = (f32[1,2048,4,64]{1,3,2,0:T(8,128)S(1)}, f32[1,2048,4,64]{1,3,2,0:T(8,128)}, u32[]{:S(2)}) copy-start(f32[1,2048,4,64]{1,3,2,0:T(8,128)} %get-tuple-element.102) | copy-start | bytes 6291460
  588.7 21.5 %all-to-all-start.5 = ((bf16[4,2,65536]{2,1,0:T(2,128)(2,1)}), bf16[4,2,65536]{2,1,0:T(2,128)(2,1)}, u32[]{:S(2)}, u32[]{:S(2)}) async-start(bf16[4,2,65536]{2,1,0:T(2,128)(2,1)} %reshape.295), calls=%async_computation.5 | async-start | bytes 2097152 | tf_op jit(solution)/shard_map/all_to_all | solution.py:257
  593.1 21.3 %copy-start.4 = (f32[1,2048,4,64]{1,3,2,0:T(8,128)S(1)}, f32[1,2048,4,64]{1,3,2,0:T(8,128)}, u32[]{:S(2)}) copy-start(f32[1,2048,4,64]{1,3,2,0:T(8,128)} %get-tuple-element.103) | copy-start | bytes 6291460
  610.2 25.1 %all-to-all-start.6 = ((bf16[4,2,65536]{2,1,0:T(2,128)(2,1)}), bf16[4,2,65536]{2,1,0:T(2,128)(2,1)}, u32[]{:S(2)}, u32[]{:S(2)}) async-start(bf16[4,2,65536]{2,1,0:T(2,128)(2,1)} %reshape.293), calls=%async_computation.6 | async-start | bytes 2097152 | tf_op jit(solution)/shard_map/all_to_all | solution.py:258
  614.4 25.1 %copy-start.10 = (bf16[1,512,1024]{2,1,0:T(8,128)(2,1)S(1)}, bf16[1,512,1024]{2,1,0:T(8,128)(2,1)}, u32[]{:S(2)}) copy-start(bf16[1,512,1024]{2,1,0:T(8,128)(2,1)} %param.22) | copy-start | bytes 3145732
  615.6 24.2 %copy-start.30 = (f32[4096]{0:T(1024)S(1)}, f32[4096]{0:T(1024)}, u32[]{:S(2)}) copy-start(f32[4096]{0:T(1024)} %get-tuple-element.365) | copy-start | bytes 49156
  635.3 18.8 %all-to-all-start.7 = ((bf16[4,2,65536]{2,1,0:T(2,128)(2,1)}), bf16[4,2,65536]{2,1,0:T(2,128)(2,1)}, u32[]{:S(2)}, u32[]{:S(2)}) async-start(bf16[4,2,65536]{2,1,0:T(2,128)(2,1)} %reshape.291), calls=%async_computation.7 | async-start | bytes 2097152 | tf_op jit(solution)/shard_map/all_to_all | solution.py:259
  639.5 160.7 %reduce-scatter.18.cloned.1.call-start = ((), (), s32[]{:S(2)}) async-start(), calls=%async_computation.21 | async-start | bytes 540672
  648.3 17.1 copy-start.28
  648.3 17.1 copy-start.29
  648.3 17.1 copy-start.32
  648.3 17.1 copy-start.39
  648.3 17.1 copy-start.40
  648.3 18.3 %copy-start.8 = (bf16[1,512,4,1,256]{1,4,2,3,0:T(8,128)(2,1)S(1)}, bf16[1,512,4,1,256]{1,4,2,3,0:T(8,128)(2,1)}, u32[]{:S(2)}) copy-start(bf16[1,512,4,1,256]{1,4,2,3,0:T(8,128)(2,1)} %copy.175) | copy-start | bytes 3145732
  648.3 18.3 %copy-start.12 = (f32[512,1024]{1,0:T(8,128)S(1)}, f32[512,1024]{1,0:T(8,128)}, u32[]{:S(2)}) copy-start(f32[512,1024]{1,0:T(8,128)} %copy-done.11) | copy-start | bytes 6291460
  666.6 276.4 %reduce-scatter.10.cloned.1.call-start = ((), (), s32[]{:S(2)}) async-start(), calls=%async_computation.17 | async-start | bytes 4325376 | tf_op jit(solution)/shard_map/reduce_scatter | solution.py:279
  670.0 433.0 %reduce-scatter.16.cloned.1.call-start = ((), (), s32[]{:S(2)}) async-start(), calls=%async_computation.20 | async-start | bytes 12976128 | tf_op jit(solution)/shard_map/reduce_scatter | solution.py:278
  693.0 769.6 %reduce-scatter.12.cloned.1.call-start = ((), (), s32[]{:S(2)}) async-start(), calls=%async_computation.18 | async-start | bytes 17301504 | tf_op jit(solution)/shard_map/reduce_scatter | solution.py:280
  705.1 1117.1 %reduce-scatter.14.cloned.1.call-start = ((), (), s32[]{:S(2)}) async-start(), calls=%async_computation.19 | async-start | bytes 17301504 | tf_op jit(solution)/shard_map/reduce_scatter | solution.py:281
  719.2 81.9 %copy-start.23 = (f32[12,32]{1,0:T(8,128)S(1)}, f32[12,32]{1,0:T(8,128)}, u32[]{:S(2)}) copy-start(f32[12,32]{1,0:T(8,128)} %param.35) | copy-start | bytes 4612
  719.2 81.9 %copy-start.35 = (f32[12,32]{1,0:T(8,128)S(1)}, f32[12,32]{1,0:T(8,128)}, u32[]{:S(2)}) copy-start(f32[12,32]{1,0:T(8,128)} %param.37) | copy-start | bytes 4612
  719.2 383.8 %copy-start.19 = (f32[32,3072]{1,0:T(8,128)S(1)}, f32[32,3072]{1,0:T(8,128)}, u32[]{:S(2)}) copy-start(f32[32,3072]{1,0:T(8,128)} %param.23) | copy-start | bytes 1179652
  727.5 1094.7 %copy-start.15 = (f32[128,1024]{1,0:T(8,128)S(1)}, f32[128,1024]{1,0:T(8,128)}, u32[]{:S(2)}) copy-start(f32[128,1024]{1,0:T(8,128)} %param.32) | copy-start | bytes 1572868
  727.5 1094.7 %copy-start.20 = (f32[128,1024]{1,0:T(8,128)S(1)}, f32[128,1024]{1,0:T(8,128)}, u32[]{:S(2)}) copy-start(f32[128,1024]{1,0:T(8,128)} %param.34) | copy-start | bytes 1572868
  727.5 1094.7 %copy-start.21 = (f32[128,1024]{1,0:T(8,128)S(1)}, f32[128,1024]{1,0:T(8,128)}, u32[]{:S(2)}) copy-start(f32[128,1024]{1,0:T(8,128)} %param.33) | copy-start | bytes 1572868
  (19 other events, 84.7 us)
Sparse Core Ops, SparseCore 0:
  11.5 72.6 all-gather.5
  87.8 55.2 all-gather.7
  146.6 76.1 all-gather.9
  226.2 83.4 all-gather.11
  666.7 133.5 reduce-scatter.17
  802.5 140.4 reduce-scatter.9
  950.1 152.9 reduce-scatter.15
  1105.3 357.1 reduce-scatter.11
  1464.9 357.3 reduce-scatter.13
where the time goes:
time: 1840 us; the launch traced here: 1830 us
  waiting for transfers between devices  1160 us (63%)
  matrix products  294 us (16%)
  other arithmetic  131 us (7%)
  local copies, waits for them, and re-layouts  128 us (7%)
  blocking collectives  71.3 us (4%)
  starting transfers between devices  33.6 us (2%)
    reduce_scatter x1, waiting for transfers between devices, body(): lax.psum_scatter(expand_grad, ('seq', 'shard'), scatter_dimension=0, tile...  357 us
    reduce_scatter x1, waiting for transfers between devices, body(): lax.psum_scatter(reduce_grad, ('seq', 'shard'), scatter_dimension=0, tile...  357 us
    reduce_scatter x1, waiting for transfers between devices, body(): lax.psum_scatter(entry_grad, ('seq', 'shard'), scatter_dimension=0, tiled...  158 us
    reduce_scatter x1, waiting for transfers between devices, body(): lax.psum_scatter(exit_grad, ('seq', 'shard'), scatter_dimension=0, tiled=...  141 us
    unnamed x10, waiting for transfers between devices  72.9 us
    all_gather x1, blocking collectives, body(): lax.all_gather(vectors.astype(jnp.bfloat16), ('seq', 'shard'), axis=1, ti...  71.3 us
    unnamed x94, local copies, waits for them, and re-layouts  52.1 us
    unnamed x7, other arithmetic  48.2 us
  transfers between devices with their start and end apart: 17, of which 11 were waited for; matrix products, arithmetic and copies ran while one was open for 14% of the time, Pallas kernels for 0%

commit v1 on v0

v1 whole, which is shorter than its diff:
```python
import math

import jax
import jax.numpy as jnp
from jax import lax
from jax.experimental import pallas as pl
from jax.experimental.pallas import tpu as pltpu
from jax.sharding import PartitionSpec as P

HEAD_DIM = 64
QBLK = 256
VMEM_BYTES = 56 * 1024 * 1024
STEP = 10


NORM_EPS = 1e-05
ADAM_EPS = 1e-06
DECAY_ONE = 0.9
DECAY_TWO = 0.999


def norm_forward(summed, gain_row, shift_row):
    centre = jnp.mean(summed, axis=-1, keepdims=True)
    centred = summed - centre
    inverse = lax.rsqrt(jnp.mean(centred * centred, axis=-1, keepdims=True) + NORM_EPS)
    normed = centred * inverse
    return (normed * gain_row + shift_row, normed, inverse)


def norm_backward(upstream, normed, inverse, gain_row):
    gain_grad = jnp.sum(upstream * normed, axis=0)
    shift_grad = jnp.sum(upstream, axis=0)
    scaled = upstream * gain_row
    bracket = (
        scaled
        - jnp.mean(scaled, axis=-1, keepdims=True)
        - normed * jnp.mean(scaled * normed, axis=-1, keepdims=True)
    )
    return (inverse * bracket, gain_grad, shift_grad)


def dot_nt(left, right):
    return lax.dot_general(left, right, (((1,), (1,)), ((), ())), preferred_element_type=jnp.float32)


def dot_nn(left, right):
    return jnp.dot(left, right, preferred_element_type=jnp.float32)


def forward_kernel(q_ref, k_ref, vt_ref, out_ref, log_ref):
    heads = q_ref.shape[1] // HEAD_DIM
    parts = []
    for head in range(heads):
        cols = slice(head * HEAD_DIM, (head + 1) * HEAD_DIM)
        query = q_ref[:, cols] * jnp.bfloat16(0.125)
        scores = dot_nt(k_ref[:, cols], query)
        highest = jnp.max(scores, axis=0, keepdims=True)
        powers = jnp.exp(scores - highest)
        total = jnp.sum(powers, axis=0, keepdims=True)
        weights = (powers * (1.0 / total)).astype(jnp.bfloat16)
        parts.append(dot_nn(vt_ref[cols, :], weights))
        log_ref[head : head + 1, :] = highest + jnp.log(total)
    out_ref[...] = jnp.concatenate(parts, axis=0).T.astype(jnp.bfloat16)


def attend_forward(packed, slot_width):
    length = packed.shape[0]
    heads = slot_width // HEAD_DIM
    values_t = packed[:, 2 * slot_width :].T
    flops = 4 * length * length * slot_width
    return pl.pallas_call(
        forward_kernel,
        grid=(length // QBLK,),
        in_specs=[
            pl.BlockSpec((QBLK, slot_width), lambda i: (i, 0)),
            pl.BlockSpec((length, slot_width), lambda i: (0, 1)),
            pl.BlockSpec((slot_width, length), lambda i: (0, 0)),
        ],
        out_specs=[
            pl.BlockSpec((QBLK, slot_width), lambda i: (i, 0)),
            pl.BlockSpec((heads, QBLK), lambda i: (0, i)),
        ],
        out_shape=[
            jax.ShapeDtypeStruct((length, slot_width), jnp.bfloat16),
            jax.ShapeDtypeStruct((heads, length), jnp.float32),
        ],
        compiler_params=pltpu.CompilerParams(vmem_limit_bytes=VMEM_BYTES),
        cost_estimate=pl.CostEstimate(
            flops=4 * flops,
            bytes_accessed=8 * length * slot_width,
            transcendentals=heads * length * length,
        ),
    )(packed, packed, values_t)


def backward_kernel(q_ref, k_ref, v_ref, kt_ref, up_ref, log_ref, out_ref, key_sum, value_sum):
    step = pl.program_id(0)
    width = q_ref.shape[1]
    heads = width // HEAD_DIM

    @pl.when(step == 0)
    def _():
        key_sum[...] = jnp.zeros_like(key_sum)
        value_sum[...] = jnp.zeros_like(value_sum)

    parts = []
    for head in range(heads):
        cols = slice(head * HEAD_DIM, (head + 1) * HEAD_DIM)
        query = q_ref[:, cols] * jnp.bfloat16(0.125)
        upstream = up_ref[:, cols]
        scores = dot_nt(k_ref[:, cols], query)
        weights = jnp.exp(scores - log_ref[head : head + 1, :])
        weight_grad = dot_nt(v_ref[:, cols], upstream)
        value_sum[:, cols] += dot_nn(weights.astype(jnp.bfloat16), upstream)
        centre = jnp.sum(weights * weight_grad, axis=0, keepdims=True)
        score_grad = (weights * (weight_grad - centre)).astype(jnp.bfloat16)
        key_sum[:, cols] += dot_nn(score_grad, query)
        parts.append(dot_nn(kt_ref[cols, :], score_grad))
    query_grad = jnp.concatenate(parts, axis=0).T * 0.125
    rows = pl.ds(pl.multiple_of(step * QBLK, QBLK), QBLK)
    out_ref[rows, 0:width] = query_grad.astype(jnp.bfloat16)

    @pl.when(step == pl.num_programs(0) - 1)
    def _():
        out_ref[:, width : 2 * width] = key_sum[...].astype(jnp.bfloat16)
        out_ref[:, 2 * width : 3 * width] = value_sum[...].astype(jnp.bfloat16)


def attend_backward(packed, log_total, upstream, slot_width):
    length = packed.shape[0]
    heads = slot_width // HEAD_DIM
    keys_t = packed[:, slot_width : 2 * slot_width].T
    flops = 10 * length * length * slot_width
    return pl.pallas_call(
        backward_kernel,
        grid=(length // QBLK,),
        in_specs=[
            pl.BlockSpec((QBLK, slot_width), lambda i: (i, 0)),
            pl.BlockSpec((length, slot_width), lambda i: (0, 1)),
            pl.BlockSpec((length, slot_width), lambda i: (0, 2)),
            pl.BlockSpec((slot_width, length), lambda i: (0, 0)),
            pl.BlockSpec((QBLK, slot_width), lambda i: (i, 0)),
            pl.BlockSpec((heads, QBLK), lambda i: (0, i)),
        ],
        out_specs=pl.BlockSpec((length, 3 * slot_width), lambda i: (0, 0)),
        out_shape=jax.ShapeDtypeStruct((length, 3 * slot_width), jnp.bfloat16),
        scratch_shapes=[
            pltpu.VMEM((length, slot_width), jnp.float32),
            pltpu.VMEM((length, slot_width), jnp.float32),
        ],
        compiler_params=pltpu.CompilerParams(vmem_limit_bytes=VMEM_BYTES),
        cost_estimate=pl.CostEstimate(
            flops=4 * flops,
            bytes_accessed=16 * length * slot_width,
            transcendentals=heads * length * length,
        ),
    )(packed, packed, packed, keys_t, upstream, log_total)


def axis_bits(axis):
    count = lax.axis_size(axis)
    return [(axis, bit) for bit in range(count.bit_length() - 1)]


def swap_bit(tensor, axis, bit):
    pairs = [(i, i ^ (1 << bit)) for i in range(lax.axis_size(axis))]
    return lax.ppermute(tensor, axis, pairs)


class Scatter:
    def __init__(self, grad, order):
        names = axis_bits("seq")[::-1] + axis_bits("shard")[::-1]
        rows, cols = grad.shape
        owners = 2 ** len(names)
        self.left = names
        self.order = order
        self.wire = grad.dtype
        self.part = grad.reshape((2,) * len(names) + (rows // owners, cols))

    def stage(self):
        axis, bit = self.order[0]
        self.order = self.order[1:]
        dim = self.left.index((axis, bit))
        self.left = self.left[:dim] + self.left[dim + 1 :]
        mine = (lax.axis_index(axis) >> bit) & 1
        keep = lax.dynamic_index_in_dim(self.part, mine, dim, keepdims=False)
        send = lax.dynamic_index_in_dim(self.part, 1 - mine, dim, keepdims=False)
        total = keep.astype(jnp.float32) + swap_bit(send, axis, bit).astype(jnp.float32)
        self.part = total.astype(self.wire) if self.order else total

    def finish(self):
        while self.order:
            self.stage()
        return self.part


def gather_vectors(rows):
    held = rows[None]
    for axis, bit in axis_bits("shard") + axis_bits("seq"):
        other = swap_bit(held, axis, bit)
        high = ((lax.axis_index(axis) >> bit) & 1) == 1
        first = jnp.where(high, other, held)
        second = jnp.where(high, held, other)
        held = jnp.concatenate([first, second], axis=0)
    return jnp.moveaxis(held, 0, 1).reshape(rows.shape[0], -1)


def adam_step(weight, drift_old, power_old, gradient, step_rate, decay_rate):
    drift_new = DECAY_ONE * drift_old + (1.0 - DECAY_ONE) * gradient
    power_new = DECAY_TWO * power_old + (1.0 - DECAY_TWO) * gradient * gradient
    normalized = (
        drift_new
        / (1.0 - DECAY_ONE**STEP)
        / (jnp.sqrt(power_new / (1.0 - DECAY_TWO**STEP)) + ADAM_EPS)
    )
    return (drift_new, power_new, weight - step_rate * (normalized + decay_rate * weight))


def body(
    tokens,
    cotangent,
    entry_weight,
    entry_drift,
    entry_power,
    exit_weight,
    exit_drift,
    exit_power,
    expand_weight,
    expand_drift,
    expand_power,
    reduce_weight,
    reduce_drift,
    reduce_power,
    vectors,
    vectors_drift,
    vectors_power,
):
    entry_low, exit_low, expand_low, reduce_low, vector_low = (
        lax.all_gather(entry_weight.astype(jnp.bfloat16), ("seq", "shard"), axis=0, tiled=True),
        lax.all_gather(exit_weight.astype(jnp.bfloat16), ("seq", "shard"), axis=0, tiled=True),
        lax.all_gather(expand_weight.astype(jnp.bfloat16), ("seq", "shard"), axis=0, tiled=True),
        lax.all_gather(reduce_weight.astype(jnp.bfloat16), ("seq", "shard"), axis=0, tiled=True),
        gather_vectors(vectors.astype(jnp.bfloat16)),
    )
    vector_rows = vector_low.astype(jnp.float32)
    seq_count, local_len, width = tokens.shape
    assert seq_count == 1
    row_count = local_len
    groups = lax.axis_size("seq")
    slot_width = width // groups
    inputs = tokens.reshape(row_count, width)

    def to_slots(matrix, blocks):
        shaped = matrix.reshape(row_count, blocks, groups, slot_width)
        sent = jnp.transpose(shaped, (2, 0, 1, 3)).reshape(groups, row_count, blocks * slot_width)
        got = lax.all_to_all(sent, "seq", split_axis=0, concat_axis=0, tiled=True)
        return got.reshape(groups * row_count, blocks * slot_width)

    def from_slots(matrix, blocks):
        sent = matrix.reshape(groups, row_count, blocks * slot_width)
        got = lax.all_to_all(sent, "seq", split_axis=0, concat_axis=0, tiled=True)
        shaped = got.reshape(groups, row_count, blocks, slot_width)
        return jnp.transpose(shaped, (1, 2, 0, 3)).reshape(row_count, blocks * width)

    bias_entry = jnp.concatenate([vector_rows[0], jnp.zeros((width,), jnp.float32), vector_rows[1]])
    projected = (
        jnp.dot(inputs, entry_low, preferred_element_type=jnp.float32) + bias_entry
    ).astype(jnp.bfloat16)
    packed = to_slots(projected, 3)
    context_heads, log_total = attend_forward(packed, slot_width)
    context = from_slots(context_heads, 1)
    attended = jnp.dot(context, exit_low, preferred_element_type=jnp.float32) + vector_rows[2]
    first_sum = inputs.astype(jnp.float32) + attended
    mixed_rows, normed_one, inverse_one = norm_forward(first_sum, vector_rows[3], vector_rows[4])
    mixed_low = mixed_rows.astype(jnp.bfloat16)
    pre_act = jnp.dot(mixed_low, expand_low, preferred_element_type=jnp.float32) + vector_rows[
        8:
    ].reshape(-1)
    normal_cdf = 0.5 + 0.5 * lax.erf(pre_act * math.sqrt(0.5))
    slope = normal_cdf + pre_act * jnp.exp(-0.5 * pre_act * pre_act) * (1.0 / math.sqrt(2.0 * math.pi))
    act_low = (pre_act * normal_cdf).astype(jnp.bfloat16)
    branch = jnp.dot(act_low, reduce_low, preferred_element_type=jnp.float32) + vector_rows[5]
    second_sum = mixed_rows + branch
    result, normed_two, inverse_two = norm_forward(second_sum, vector_rows[6], vector_rows[7])
    block_out = result.astype(jnp.bfloat16).reshape(tokens.shape)
    upstream = cotangent.reshape(row_count, width).astype(jnp.float32)
    second_grad, gain_two, shift_two = norm_backward(
        upstream, normed_two, inverse_two, vector_rows[6]
    )
    branch_grad = second_grad.astype(jnp.bfloat16)
    across = [("seq", 0)] + axis_bits("seq")[1:] + axis_bits("shard")
    along = [("seq", 0)] + axis_bits("shard") + axis_bits("seq")[1:]
    reduce_grad = jnp.einsum(
        "rf,rd->fd", act_low, branch_grad, preferred_element_type=jnp.float32
    ).astype(jnp.bfloat16)
    reduce_grad, branch_grad = lax.optimization_barrier((reduce_grad, branch_grad))
    reduce_sum = Scatter(reduce_grad, across)
    reduce_sum.stage()
    branch_bias = jnp.sum(branch_grad.astype(jnp.float32), axis=0)
    act_grad = jnp.einsum("rd,fd->rf", branch_grad, reduce_low, preferred_element_type=jnp.float32)
    pre_grad = (act_grad * slope).astype(jnp.bfloat16)
    expand_grad = jnp.einsum(
        "rd,rf->df", mixed_low, pre_grad, preferred_element_type=jnp.float32
    ).astype(jnp.bfloat16)
    expand_grad, pre_grad = lax.optimization_barrier((expand_grad, pre_grad))
    expand_sum = Scatter(expand_grad, along)
    expand_sum.stage()
    expand_bias = jnp.sum(pre_grad.astype(jnp.float32), axis=0).reshape(4, width)
    mixed_grad = second_grad + jnp.einsum(
        "rf,df->rd", pre_grad, expand_low, preferred_element_type=jnp.float32
    )
    vector_back = jnp.concatenate(
        [branch_bias[None], gain_two[None], shift_two[None], expand_bias], axis=0
    )
    first_grad, gain_one, shift_one = norm_backward(
        mixed_grad, normed_one, inverse_one, vector_rows[3]
    )
    attended_grad = first_grad.astype(jnp.bfloat16)
    exit_grad = jnp.einsum(
        "rc,rd->cd", context, attended_grad, preferred_element_type=jnp.float32
    ).astype(jnp.bfloat16)
    exit_bias = jnp.sum(attended_grad.astype(jnp.float32), axis=0)
    context_grad = jnp.einsum(
        "rd,cd->rc", attended_grad, exit_low, preferred_element_type=jnp.float32
    ).astype(jnp.bfloat16)
    exit_sum = Scatter(exit_grad, across)
    exit_sum.stage()
    heads_grad = to_slots(context_grad, 1)
    heads_grad, reduce_sum.part, expand_sum.part, exit_sum.part = lax.optimization_barrier(
        (heads_grad, reduce_sum.part, expand_sum.part, exit_sum.part)
    )
    packed_grad = attend_backward(packed, log_total, heads_grad, slot_width)
    for running in (reduce_sum, expand_sum):
        running.stage()
    packed_grad, reduce_sum.part, expand_sum.part = lax.optimization_barrier(
        (packed_grad, reduce_sum.part, expand_sum.part)
    )
    entry_back = from_slots(packed_grad, 3)
    entry_grad = jnp.einsum(
        "rd,re->de", inputs, entry_back, preferred_element_type=jnp.float32
    ).astype(jnp.bfloat16)
    entry_grad, entry_back = lax.optimization_barrier((entry_grad, entry_back))
    half = entry_grad.shape[1] // 2
    entry_sums = (Scatter(entry_grad[:, :half], across), Scatter(entry_grad[:, half:], along))
    bias_sums = jnp.sum(entry_back.astype(jnp.float32), axis=0)
    input_grad = first_grad + jnp.einsum(
        "re,de->rd", entry_back, entry_low, preferred_element_type=jnp.float32
    )
    vector_front = jnp.stack(
        [bias_sums[:width], bias_sums[2 * width :], exit_bias, gain_one, shift_one], axis=0
    )
    vector_grad = jnp.concatenate([vector_front, vector_back], axis=0)
    owners = groups * lax.axis_size("shard")
    own_cols = width // owners
    vector_grad = vector_grad.reshape(-1, owners, own_cols)
    vector_grad = jnp.moveaxis(vector_grad, 0, 1).reshape(owners, -1)
    summed_vectors = Scatter(vector_grad, across).finish().reshape(-1, own_cols)
    summed_reduce = reduce_sum.finish()
    summed_expand = expand_sum.finish()
    summed_exit = exit_sum.finish()
    summed_entry = jnp.concatenate([running.finish() for running in entry_sums], axis=1)
    entry_new = adam_step(entry_weight, entry_drift, entry_power, summed_entry, 0.03, 0.01)
    exit_new = adam_step(exit_weight, exit_drift, exit_power, summed_exit, 0.3, 0.01)
    expand_new = adam_step(expand_weight, expand_drift, expand_power, summed_expand, 0.03, 0.01)
    reduce_new = adam_step(reduce_weight, reduce_drift, reduce_power, summed_reduce, 0.02, 0.01)
    vectors_new = adam_step(vectors, vectors_drift, vectors_power, summed_vectors, 0.2, 0.0)
    return (
        block_out,
        input_grad.reshape(tokens.shape),
        entry_new[0],
        entry_new[1],
        entry_new[2],
        exit_new[0],
        exit_new[1],
        exit_new[2],
        expand_new[0],
        expand_new[1],
        expand_new[2],
        reduce_new[0],
        reduce_new[1],
        reduce_new[2],
        vectors_new[0],
        vectors_new[1],
        vectors_new[2],
    )


def solution(mesh):
    in_specs = (
        P("shard", "seq", None),
        P("shard", "seq", None),
        P(("seq", "shard"), None),
        P(("seq", "shard"), None),
        P(("seq", "shard"), None),
        P(("seq", "shard"), None),
        P(("seq", "shard"), None),
        P(("seq", "shard"), None),
        P(("seq", "shard"), None),
        P(("seq", "shard"), None),
        P(("seq", "shard"), None),
        P(("seq", "shard"), None),
        P(("seq", "shard"), None),
        P(("seq", "shard"), None),
        P(None, ("seq", "shard")),
        P(None, ("seq", "shard")),
        P(None, ("seq", "shard")),
    )
    out_specs = (
        P("shard", "seq", None),
        P("shard", "seq", None),
        P(("seq", "shard"), None),
        P(("seq", "shard"), None),
        P(("seq", "shard"), None),
        P(("seq", "shard"), None),
        P(("seq", "shard"), None),
        P(("seq", "shard"), None),
        P(("seq", "shard"), None),
        P(("seq", "shard"), None),
        P(("seq", "shard"), None),
        P(("seq", "shard"), None),
        P(("seq", "shard"), None),
        P(("seq", "shard"), None),
        P(None, ("seq", "shard")),
        P(None, ("seq", "shard")),
        P(None, ("seq", "shard")),
    )
    return jax.shard_map(body, mesh=mesh, in_specs=in_specs, out_specs=out_specs, check_vma=False)
```

time: 1840 us -> 685 us (0.37)
  waiting for transfers between devices: 1160 us -> 235 us
  matrix products: 294 us -> 81.1 us
  Pallas kernels: 0 us -> 108 us
  other arithmetic: 131 us -> 52.9 us
  local copies, waits for them, and re-layouts: 128 us -> 86.2 us
  blocking collectives: 71.3 us -> 46.1 us
    reduce_scatter x4 -> x0, waiting for transfers between devices: 1010 us -> none  [the longest x1 357 us: body(): lax.psum_scatter(expand_grad, ('seq', 'shard'), scatter_dimension=0, tile...]
    dot_general x28 -> x0, matrix products: 174 us -> none  [the longest x4 40.3 us: one_block(): jnp.einsum('sqhd,skhd->shqk', upstream_block, value_rows, preferred_eleme...]
    pallas_call x0 -> x2, Pallas kernels: none -> 108 us  [the longest x1 58.4 us: attend_backward(): pl.pallas_call(backward_kernel, grid=(length // QBLK,), in_specs=[pl.Bloc...]
    ppermute x0 -> x35, waiting for transfers between devices: none -> 98.4 us  [swap_bit(): return lax.ppermute(tensor, axis, pairs)]
    unnamed x10 -> x4, waiting for transfers between devices: 72.9 us -> 0.07 us
    all_gather x1 -> x0, blocking collectives: 71.3 us -> none  [body(): lax.all_gather(vectors.astype(jnp.bfloat16), ('seq', 'shard'), axis=1, ti...]
    all_gather x1, waiting for transfers between devices: 0.02 us -> 70 us  [body(): lax.all_gather(reduce_weight.astype(jnp.bfloat16), ('seq', 'shard'), axis...]
    all_to_all x8 -> x3, waiting for transfers between devices: 73.3 us -> 16 us  [the longest x2 16 us: from_slots(): got = lax.all_to_all(sent, 'seq', split_axis=0, concat_axis=0, tiled=True)]
  transfers between devices with their start and end apart: 17 -> 42, of which waited for: 11 -> 20; matrix products, arithmetic and copies ran while one was open for 14% -> 24% of each run, Pallas kernels for 0% -> 16%
where the time goes in v1:
time: 685 us; the launch traced here: 676 us
  waiting for transfers between devices  235 us (34%)
  Pallas kernels  108 us (16%)
  local copies, waits for them, and re-layouts  86.2 us (13%)
  matrix products  81.1 us (12%)
  other arithmetic  52.9 us (8%)
  starting transfers between devices  51.5 us (8%)
  blocking collectives  46.1 us (7%)
  between operations  15 us (2%)
    ppermute x35, waiting for transfers between devices, swap_bit(): return lax.ppermute(tensor, axis, pairs)  98.4 us
    all_gather x1, waiting for transfers between devices, body(): lax.all_gather(reduce_weight.astype(jnp.bfloat16), ('seq', 'shard'), axis...  70 us
    pallas_call x1, Pallas kernels, attend_backward(): pl.pallas_call(backward_kernel, grid=(length // QBLK,), in_specs=[pl.Bloc...  58.4 us
    all_gather x1, waiting for transfers between devices, body(): lax.all_gather(entry_weight.astype(jnp.bfloat16), ('seq', 'shard'), axis=...  50.7 us
    pallas_call x1, Pallas kernels, attend_forward(): pl.pallas_call(forward_kernel, grid=(length // QBLK,), in_specs=[pl.Block...  49.8 us
    all_to_all x1, blocking collectives, to_slots(): got = lax.all_to_all(sent, 'seq', split_axis=0, concat_axis=0, tiled=True)  46.1 us
    ppermute x35, starting transfers between devices, swap_bit(): return lax.ppermute(tensor, axis, pairs)  39.9 us
    convert_element_type x20, other arithmetic, stage(): self.part = total.astype(self.wire) if self.order else total  33.8 us
  transfers between devices with their start and end apart: 42, of which 20 were waited for; matrix products, arithmetic and copies ran while one was open for 24% of the time, Pallas kernels for 16%

profile of v1, /device:TPU:0, one launch (start us, length us, event | category | flops | bytes accessed | tf_op | source)
XLA Modules:
  0.0 676.2 jit_solution(13485742261627864346)
XLA Ops:
  13.4 3.0 collective-permute-start
  21.8 3.1 collective-permute-start.2
  33.1 50.7 %all-gather.5.cloned.1.call-done = bf16[1024,3072]{1,0:T(8,128)(2,1)} async-done(((bf16[32,3072]{1,0:T(8,128)(2,1)}), bf16[1024,3072]{1,0:T(8,128)(2,1)}) %all-gather.5.cloned.1.call-update) | async-done | bytes 6291472 | tf_op jit(solution)/shard_map/all_gather | solution.py:239
  83.9 7.6 %add_convert_fusion = bf16[512,3072]{1,0:T(8,128)(2,1)} fusion(bf16[1024,3072]{1,0:T(8,128)(2,1)} %all-gather.5.cloned.1.call-done, f32[3072]{0:T(1024)S(1)} %pad_maximum_fusion.4, bf16[1,512,1024]{2,1,0:T(8,128)(2,1)S(1)} %copy-done.25), kind=kOutput, calls=%fused_computation.18 | convolution fusion | flops 3224371200 | bytes 10498048 | tf_op jit(solution)/shard_map/dot_general | solution.py:267
  91.4 5.5 reshape.244
  96.9 4.3 copy.94
  101.2 46.1 %all_to_all.20 = bf16[4,512,768]{1,2,0:T(8,128)(2,1)S(1)} all-to-all(bf16[4,512,768]{1,2,0:T(8,128)(2,1)} %bitcast.276), channel_id=1, replica_groups=mesh['seq'=4,'shard'=8] {'seq'}, dimensions={0} | all-to-all | bytes 6291456 | tf_op jit(solution)/shard_map/all_to_all | solution.py:256
  147.8 2.8 copy.96.q_ref.k_ref.v_ref
  152.1 49.8 %shard_map.296 = (bf16[2048,256]{1,0:T(8,128)(2,1)}, f32[4,2048]{1,0:T(4,128)}) custom-call(bf16[2048,768]{1,0:T(8,128)(2,1)} %copy.96.q_ref.k_ref.v_ref, bf16[2048,768]{1,0:T(8,128)(2,1)} %copy.96.q_ref.k_ref.v_ref, bf16[256,2048]{1,0:T(8,128)(2,1)} %get-tuple-element.88.vt_ref), custom_call_target="tpu_custom_call" | custom-call | flops 17179869184 | bytes 4194304 | tf_op jit(solution)/shard_map/pallas_call | solution.py:71
  204.2 4.0 all-to-all-start.1
  208.7 16.0 %all-to-all-done.1 = bf16[4,512,256]{1,2,0:T(8,128)(2,1)S(1)} async-done(((bf16[4,512,256]{1,2,0:T(8,128)(2,1)}), bf16[4,512,256]{1,2,0:T(8,128)(2,1)S(1)}, u32[]{:S(2)}, u32[]{:S(2)}) %all-to-all-start.1) | async-done | bytes 1048608 | tf_op jit(solution)/shard_map/all_to_all | solution.py:261
  224.7 3.7 fusion.70
  228.9 10.4 %multiply_convert_fusion = (bf16[512,4096]{1,0:T(8,128)(2,1)}, f32[512,4096]{1,0:T(8,128)}) fusion(f32[4096]{0:T(1024)S(1)} %add.378, bf16[1024,4096]{1,0:T(8,128)(2,1)} %all-gather.9.cloned.1.call-done, f32[512,1024]{1,0:T(8,128)S(1)} %get-tuple-element.106, f32[1024]{0:T(1024)S(1)} %add.375, f32[1024]{0:T(1024)S(1)} %mul.325, ...), kind=kOutput, calls=%fused_computation.12 | convolution fusion | flops 4310171648 | bytes 23097344 | tf_op jit(solution)/shard_map/dot_general | solution.py:276
  239.3 70.0 %all-gather.11.cloned.1.call-done = bf16[4096,1024]{1,0:T(8,128)(2,1)} async-done(((bf16[128,1024]{1,0:T(8,128)(2,1)}), bf16[4096,1024]{1,0:T(8,128)(2,1)}) %all-gather.11.cloned.1.call-update) | async-done | bytes 8388624 | tf_op jit(solution)/shard_map/all_gather | solution.py:242
  309.4 8.4 %fusion.71 = (f32[512]{0:T(512)S(1)}, f32[512,1024]{1,0:T(8,128)S(1)}) fusion(f32[1024]{0:T(1024)S(1)} %add.382, bf16[512,4096]{1,0:T(8,128)(2,1)} %get-tuple-element.107, bf16[4096,1024]{1,0:T(8,128)(2,1)} %all-gather.11.cloned.1.call-done, f32[1024]{0:T(1024)S(1)} %add.375, f32[1024]{0:T(1024)S(1)} %mul.325, f32[512]{0:T(512)S(1)} %add_rsqrt_fusion.1, ...), kind=kOutput, calls=%fused_computation.226 | convolution fusion | flops 4298636800 | bytes 16795648 | tf_op jit(solution)/shard_map/dot_general | solution.py:282
  322.5 6.8 %convolution_convert_fusion.1 = bf16[4096,1024]{1,0:T(8,128)(2,1)} fusion(bf16[512,4096]{1,0:T(8,128)(2,1)S(1)} %copy-done.41, bf16[512,1024]{1,0:T(8,128)(2,1)S(1)} %get-tuple-element.33), kind=kOutput, calls=%fused_computation.15 | convolution fusion | flops 4299161600 | bytes 13631488 | tf_op jit(solution)/shard_map/rf,rd->fd/dot_general | solution.py:293
  329.3 10.4 %fusion.5 = bf16[512,4096]{1,0:T(8,128)(2,1)S(1)} fusion(f32[512,4096]{1,0:T(8,128)} %get-tuple-element.108, bf16[512,1024]{1,0:T(8,128)(2,1)S(1)} %get-tuple-element.33, bf16[4096,1024]{1,0:T(8,128)(2,1)} %all-gather.11.cloned.1.call-done, f32[4096]{0:T(1024)S(1)} %add.378), kind=kOutput, calls=%fused_computation.6 | convolution fusion | flops 4318035968 | bytes 22036480 | tf_op jit(solution)/shard_map/rd,fd->rf/dot_general | solution.py:300
  339.7 7.2 %convolution_convert_fusion = bf16[1024,4096]{1,0:T(8,128)(2,1)} fusion(bf16[512,4096]{1,0:T(8,128)(2,1)S(1)} %fusion.5, f32[512,1024]{1,0:T(8,128)S(1)} %get-tuple-element.106, f32[1024]{0:T(1024)S(1)} %add.375, f32[1024]{0:T(1024)S(1)} %mul.325, f32[512]{0:T(512)S(1)} %add_rsqrt_fusion.1, f32[512]{0:T(512)S(1)} %broadcast_multiply_fusion.5), kind=kOutput, calls=%fused_computation.14 | convolution fusion | flops 4301783040 | bytes 14692352 | tf_op jit(solution)/shard_map/rd,rf->df/dot_general | solution.py:302
  347.0 6.9 %constant_dynamic-slice_fusion.15 = (bf16[2,1,2,2,2,128,1024]{6,5,4,3,2,1,0:T(8,128)(2,1)}, bf16[2,1,2,2,2,128,1024]{6,5,4,3,2,1,0:T(8,128)(2,1)S(1)}) fusion(bf16[2,2,2,2,2,128,1024]{6,5,4,3,2,1,0:T(8,128)(2,1)} %bitcast.280, s32[]{:T(128)S(6)} %select_n.181, s32[]{:T(128)S(6)} %select_n.182), kind=kLoop, calls=%fused_computation.186 | loop fusion | bytes 16777224 | tf_op jit(solution)/shard_map/jit(dynamic_index_in_dim)/dynamic_slice | solution.py:186
  356.9 6.3 constant_dynamic-slice_fusion.13
  365.7 8.8 %multiply_reduce_fusion = (f32[1024]{0:T(1024)S(1)}, f32[512]{0:T(512)S(1)}, f32[512]{0:T(512)S(1)}, f32[1024]{0:T(1024)S(1)}, f32[512,1024]{1,0:T(8,128)S(1)}) fusion(f32[512,1024]{1,0:T(8,128)S(1)} %get-tuple-element.106, f32[512]{0:T(512)S(1)} %add_rsqrt_fusion.1, f32[512]{0:T(512)S(1)} %broadcast_multiply_fusion.5, f32[1024]{0:T(1024)S(1)} %mul.325, ...), kind=kOutput, calls=%fused_computation.49 | convolution fusion | flops 4304401408 | bytes 19955712 | tf_op jit(solution)/shard_map/rf,df->rd/dot_general | solution.py:309
  378.8 3.5 convolution_convert_fusion.3
  384.2 3.7 all-to-all-start.2
  389.6 7.3 %fusion.6 = bf16[2,2,2,2,32,4096]{5,4,0,1,2,3:T(8,128)(2,1)} fusion(bf16[2,2,2,2,32,4096]{5,4,0,1,2,3:T(8,128)(2,1)} %collective-permute-done.6, bf16[2,1,2,2,2,32,4096]{6,5,4,3,2,1,0:T(8,128)(2,1)} %get-tuple-element.79), kind=kLoop, calls=%fused_computation.8 | loop fusion | flops 8388608 | bytes 12582912 | tf_op jit(solution)/shard_map/convert_element_type | solution.py:189
  397.0 6.3 fusion.7
  403.3 3.5 dynamic-slice_bitcast_fusion.1
  412.0 58.4 %shard_map.297 = bf16[2048,768]{1,0:T(8,128)(2,1)} custom-call(bf16[2048,768]{1,0:T(8,128)(2,1)} %copy.96.q_ref.k_ref.v_ref, bf16[2048,768]{1,0:T(8,128)(2,1)} %copy.96.q_ref.k_ref.v_ref, bf16[2048,768]{1,0:T(8,128)(2,1)} %copy.96.q_ref.k_ref.v_ref, bf16[256,2048]{1,0:T(8,128)(2,1)} %get-tuple-element.87.kt_ref, bf16[2048,256]{1,0:T(8,128)(2,1)} %bitcast.285, ...), custom_call_target="tpu_custom_call" | custom-call | flops 42949672960 | bytes 8388608 | tf_op jit(solution)/shard_map/pallas_call | solution.py:134
  471.3 3.2 fusion.9
  474.6 3.2 fusion.8
  485.6 20.9 %collective-permute-done.22 = bf16[2,32,1024]{2,1,0:T(8,128)(2,1)} collective-permute-done((bf16[2,32,1024]{2,1,0:T(8,128)(2,1)}, bf16[2,32,1024]{2,1,0:T(8,128)(2,1)}, u32[]{:S(2)}, u32[]{:S(2)}) %collective-permute-start.22) | collective-permute-done | bytes 131104 | tf_op jit(solution)/shard_map/ppermute | solution.py:167
  517.2 2.8 copy.110
  520.0 3.7 all-to-all-start.3
  523.7 10.4 %collective-permute-done.27 = bf16[2,2,128,1024]{3,2,0,1:T(8,128)(2,1)} collective-permute-done((bf16[2,2,128,1024]{3,2,0,1:T(8,128)(2,1)}, bf16[2,2,128,1024]{3,2,0,1:T(8,128)(2,1)}, u32[]{:S(2)}, u32[]{:S(2)}) %collective-permute-start.27) | collective-permute-done | bytes 1048608 | tf_op jit(solution)/shard_map/ppermute | solution.py:167
  536.7 2.8 collective-permute-done.25
  542.2 8.4 %collective-permute-done.28 = bf16[2,128,1024]{2,1,0:T(8,128)(2,1)S(1)} collective-permute-done((bf16[2,128,1024]{2,1,0:T(8,128)(2,1)S(1)}, bf16[2,128,1024]{2,1,0:T(8,128)(2,1)S(1)}, u32[]{:S(2)}, u32[]{:S(2)}) %collective-permute-start.28) | collective-permute-done | bytes 524320 | tf_op jit(solution)/shard_map/ppermute | solution.py:167
  551.6 14.6 %collective-permute-done.26 = bf16[32,4096]{1,0:T(8,128)(2,1)S(1)} collective-permute-done((bf16[32,4096]{1,0:T(8,128)(2,1)S(1)}, bf16[32,4096]{1,0:T(8,128)(2,1)S(1)}, u32[]{:S(2)}, u32[]{:S(2)}) %collective-permute-start.26) | collective-permute-done | bytes 262176 | tf_op jit(solution)/shard_map/ppermute | solution.py:167
  571.7 5.3 convert_bitcast_fusion
  579.7 3.0 multiply_subtract_fusion
  583.1 6.2 fusion.68
  589.4 4.7 copy.113
  595.1 3.3 constant_dynamic-slice_fusion.9
  599.6 4.8 copy.112
  606.1 2.8 dynamic-slice_bitcast_fusion.2
  610.3 7.6 %add_bitcast_fusion = f32[1,512,1024]{2,1,0:T(8,128)} fusion(f32[512,1024]{1,0:T(8,128)S(1)} %copy-done.18, bf16[512,3072]{0,1:T(8,128)(2,1)S(1)} %bitcast.271, bf16[1024,3072]{1,0:T(8,128)(2,1)} %all-gather.5.cloned.1.call-done), kind=kOutput, calls=%fused_computation.51 | convolution fusion | flops 3221749760 | bytes 13631488 | tf_op jit(solution)/shard_map/re,de->rd/dot_general | solution.py:346
  626.1 13.9 %collective-permute-done.16 = bf16[2,2,2,32,1536]{4,3,0,1,2:T(8,128)(2,1)S(1)} collective-permute-done((bf16[2,2,2,32,1536]{4,3,0,1,2:T(8,128)(2,1)S(1)}, bf16[2,2,2,32,1536]{4,3,0,1,2:T(8,128)(2,1)S(1)}, u32[]{:S(2)}, u32[]{:S(2)}) %collective-permute-start.16) | collective-permute-done | bytes 786464 | tf_op jit(solution)/shard_map/ppermute | solution.py:167
  644.0 6.2 collective-permute-done.17
  654.6 5.8 collective-permute-done.18
  665.2 3.0 collective-permute-done.14
  (285 shorter events, 109.7 us)
Async XLA Ops:
  7.2 76.6 %all-gather.5.cloned.1.call-start = ((), (), s32[]{:S(2)}) async-start(), calls=%async_computation.4 | async-start | bytes 6488064 | tf_op jit(solution)/shard_map/all_gather | solution.py:239
  9.0 74.9 %copy-start.25 = (bf16[1,512,1024]{2,1,0:T(8,128)(2,1)S(1)}, bf16[1,512,1024]{2,1,0:T(8,128)(2,1)}, u32[]{:S(2)}) copy-start(bf16[1,512,1024]{2,1,0:T(8,128)(2,1)} %param.17) | copy-start | bytes 3145732
  9.0 199.7 %all-gather.7.cloned.1.call-start = ((), (), s32[]{:S(2)}) async-start(), calls=%async_computation.5 | async-start | bytes 2162688 | tf_op jit(solution)/shard_map/all_gather | solution.py:240
  10.7 218.2 %all-gather.9.cloned.1.call-start = ((), (), s32[]{:S(2)}) async-start(), calls=%async_computation.6 | async-start | bytes 8650752 | tf_op jit(solution)/shard_map/all_gather | solution.py:241
  12.6 296.8 %all-gather.11.cloned.1.call-start = ((), (), s32[]{:S(2)}) async-start(), calls=%async_computation.7 | async-start | bytes 8650752 | tf_op jit(solution)/shard_map/all_gather | solution.py:242
  13.4 4.6 collective-permute-start
  18.0 3.8 collective-permute-start.1
  21.8 5.0 collective-permute-start.2
  26.9 1.3 collective-permute-start.3
  28.2 4.3 collective-permute-start.4
  204.2 20.5 %all-to-all-start.1 = ((bf16[4,512,256]{1,2,0:T(8,128)(2,1)}), bf16[4,512,256]{1,2,0:T(8,128)(2,1)S(1)}, u32[]{:S(2)}, u32[]{:S(2)}) async-start(bf16[4,512,256]{1,2,0:T(8,128)(2,1)} %copy.98), calls=%async_computation.1 | async-start | bytes 2097152 | tf_op jit(solution)/shard_map/all_to_all | solution.py:261
  356.6 40.3 %collective-permute-start.5 = (bf16[2,2,2,2,128,1024]{5,4,1,2,3,0:T(8,128)(2,1)}, bf16[2,2,2,2,128,1024]{5,4,1,2,3,0:T(8,128)(2,1)}, u32[]{:S(2)}, u32[]{:S(2)}) collective-permute-start(bf16[2,2,2,2,128,1024]{5,4,1,2,3,0:T(8,128)(2,1)} %bitcast.263), channel_id=1, source_target_pairs={{0,8},{8,0},{16,24},{24,16},{1,9},{9,1},{17,25},{25,17},{2,10},{10... | collective-permute-start | bytes 12582920 | tf_op jit(solution)/shard_map/ppermute | solution.py:167
  365.4 24.2 %collective-permute-start.6 = (bf16[2,2,2,2,32,4096]{5,4,0,1,2,3:T(8,128)(2,1)}, bf16[2,2,2,2,32,4096]{5,4,0,1,2,3:T(8,128)(2,1)}, u32[]{:S(2)}, u32[]{:S(2)}) collective-permute-start(bf16[2,2,2,2,32,4096]{5,4,0,1,2,3:T(8,128)(2,1)} %bitcast.262), channel_id=1, source_target_pairs={{0,8},{8,0},{16,24},{24,16},{1,9},{9,1},{17,25},{25,17},{2,10},{10... | collective-permute-start | bytes 12582920 | tf_op jit(solution)/shard_map/ppermute | solution.py:167
  378.3 9.7 %collective-permute-start.7 = (bf16[2,2,2,2,32,1024]{5,4,1,2,3,0:T(8,128)(2,1)}, bf16[2,2,2,2,32,1024]{5,4,1,2,3,0:T(8,128)(2,1)}, u32[]{:S(2)}, u32[]{:S(2)}) collective-permute-start(bf16[2,2,2,2,32,1024]{5,4,1,2,3,0:T(8,128)(2,1)} %bitcast.265), channel_id=1, source_target_pairs={{0,8},{8,0},{16,24},{24,16},{1,9},{9,1},{17,25},{25,17},{2,10},{10... | collective-permute-start | bytes 3145736 | tf_op jit(solution)/shard_map/ppermute | solution.py:167
  384.2 19.1 %all-to-all-start.2 = ((bf16[4,512,256]{2,1,0:T(8,128)(2,1)}), bf16[4,512,256]{2,1,0:T(8,128)(2,1)S(1)}, u32[]{:S(2)}, u32[]{:S(2)}) async-start(bf16[4,512,256]{2,1,0:T(8,128)(2,1)} %bitcast.266), calls=%async_computation.2 | async-start | bytes 2097152 | tf_op jit(solution)/shard_map/all_to_all | solution.py:256
  406.8 64.5 %collective-permute-start.8 = (bf16[2,2,2,128,1024]{4,3,0,1,2:T(8,128)(2,1)}, bf16[2,2,2,128,1024]{4,3,0,1,2:T(8,128)(2,1)}, u32[]{:S(2)}, u32[]{:S(2)}) collective-permute-start(bf16[2,2,2,128,1024]{4,3,0,1,2:T(8,128)(2,1)} %dynamic-slice_bitcast_fusion.1), channel_id=1, source_target_pairs={{0,16},{8,24},{16,0},{24,8},{1,17},{9,25},{17,1},{25,9},{2,18},{10... | collective-permute-start | bytes 6291464 | tf_op jit(solution)/shard_map/ppermute | solution.py:167
  410.4 64.2 %collective-permute-start.9 = (bf16[2,2,2,32,4096]{4,3,0,1,2:T(8,128)(2,1)}, bf16[2,2,2,32,4096]{4,3,0,1,2:T(8,128)(2,1)}, u32[]{:S(2)}, u32[]{:S(2)}) collective-permute-start(bf16[2,2,2,32,4096]{4,3,0,1,2:T(8,128)(2,1)} %dynamic-slice_bitcast_fusion), channel_id=1, source_target_pairs={{0,1},{1,0},{2,3},{3,2},{4,5},{5,4},{6,7},{7,6},{8,9},{9,8},{10,11... | collective-permute-start | bytes 6291464 | tf_op jit(solution)/shard_map/ppermute | solution.py:167
  411.9 58.5 %collective-permute-start.20 = (bf16[2,2,2,32,1024]{4,3,0,1,2:T(8,128)(2,1)S(1)}, bf16[2,2,2,32,1024]{4,3,0,1,2:T(8,128)(2,1)S(1)}, u32[]{:S(2)}, u32[]{:S(2)}) collective-permute-start(bf16[2,2,2,32,1024]{4,3,0,1,2:T(8,128)(2,1)S(1)} %dynamic-slice_bitcast_fusion.9), channel_id=1, source_target_pairs={{0,16},{8,24},{16,0},{24,8},{1,17},{9,25},{17,1},{25,9},{2,18},{10... | collective-permute-start | bytes 1572872 | tf_op jit(solution)/shard_map/ppermute | solution.py:167
  470.7 11.0 %collective-permute-start.21 = (bf16[2,2,32,1024]{3,2,0,1:T(8,128)(2,1)S(1)}, bf16[2,2,32,1024]{3,2,0,1:T(8,128)(2,1)}, u32[]{:S(2)}, u32[]{:S(2)}) collective-permute-start(bf16[2,2,32,1024]{3,2,0,1:T(8,128)(2,1)S(1)} %dynamic-slice_bitcast_fusion.14), channel_id=1, source_target_pairs={{0,1},{1,0},{2,3},{3,2},{4,5},{5,4},{6,7},{7,6},{8,9},{9,8},{10,11... | collective-permute-start | bytes 786440 | tf_op jit(solution)/shard_map/ppermute | solution.py:167
  474.6 34.8 %copy-start.5 = (bf16[2,2,2,128,1024]{4,3,0,1,2:T(8,128)(2,1)}, bf16[2,2,2,128,1024]{4,3,0,1,2:T(8,128)(2,1)S(1)}, u32[]{:S(2)}) copy-start(bf16[2,2,2,128,1024]{4,3,0,1,2:T(8,128)(2,1)S(1)} %fusion.9) | copy-start | bytes 6291460
  479.0 33.1 %collective-permute-start.24 = (bf16[2,2,32,4096]{3,2,0,1:T(8,128)(2,1)}, bf16[2,2,32,4096]{3,2,0,1:T(8,128)(2,1)}, u32[]{:S(2)}, u32[]{:S(2)}) collective-permute-start(bf16[2,2,32,4096]{3,2,0,1:T(8,128)(2,1)} %dynamic-slice_bitcast_fusion.4), channel_id=1, source_target_pairs={{0,2},{1,3},{2,0},{3,1},{4,6},{5,7},{6,4},{7,5},{8,10},{9,11},{10,... | collective-permute-start | bytes 3145736 | tf_op jit(solution)/shard_map/ppermute | solution.py:167
  483.5 23.0 %collective-permute-start.22 = (bf16[2,32,1024]{2,1,0:T(8,128)(2,1)}, bf16[2,32,1024]{2,1,0:T(8,128)(2,1)}, u32[]{:S(2)}, u32[]{:S(2)}) collective-permute-start(bf16[2,32,1024]{2,1,0:T(8,128)(2,1)} %dynamic-slice_bitcast_fusion.17), channel_id=1, source_target_pairs={{0,2},{1,3},{2,0},{3,1},{4,6},{5,7},{6,4},{7,5},{8,10},{9,11},{10,... | collective-permute-start | bytes 393224 | tf_op jit(solution)/shard_map/ppermute | solution.py:167
  485.6 26.5 %copy-start.7 = (bf16[2,2,2,32,4096]{4,3,0,1,2:T(8,128)(2,1)S(1)}, bf16[2,2,2,32,4096]{4,3,0,1,2:T(8,128)(2,1)}, u32[]{:S(2)}) copy-start(bf16[2,2,2,32,4096]{4,3,0,1,2:T(8,128)(2,1)} %copy-done.6) | copy-start | bytes 6291460
  507.5 8.9 %collective-permute-start.23 = (bf16[32,1024]{1,0:T(8,128)(2,1)S(1)}, bf16[32,1024]{1,0:T(8,128)(2,1)S(1)}, u32[]{:S(2)}, u32[]{:S(2)}) collective-permute-start(bf16[32,1024]{1,0:T(8,128)(2,1)S(1)} %dynamic-slice_bitcast_fusion.20), channel_id=1, source_target_pairs={{0,4},{1,5},{2,6},{3,7},{4,0},{5,1},{6,2},{7,3},{8,12},{9,13},{10,... | collective-permute-start | bytes 196616 | tf_op jit(solution)/shard_map/ppermute | solution.py:167
  510.5 23.6 %collective-permute-start.27 = (bf16[2,2,128,1024]{3,2,0,1:T(8,128)(2,1)}, bf16[2,2,128,1024]{3,2,0,1:T(8,128)(2,1)}, u32[]{:S(2)}, u32[]{:S(2)}) collective-permute-start(bf16[2,2,128,1024]{3,2,0,1:T(8,128)(2,1)} %dynamic-slice_bitcast_fusion.3), channel_id=1, source_target_pairs={{0,1},{1,0},{2,3},{3,2},{4,5},{5,4},{6,7},{7,6},{8,9},{9,8},{10,11... | collective-permute-start | bytes 3145736 | tf_op jit(solution)/shard_map/ppermute | solution.py:167
  515.3 24.2 %collective-permute-start.25 = (bf16[2,32,4096]{2,1,0:T(8,128)(2,1)}, bf16[2,32,4096]{2,1,0:T(8,128)(2,1)}, u32[]{:S(2)}, u32[]{:S(2)}) collective-permute-start(bf16[2,32,4096]{2,1,0:T(8,128)(2,1)} %dynamic-slice_bitcast_fusion.8), channel_id=1, source_target_pairs={{0,4},{1,5},{2,6},{3,7},{4,0},{5,1},{6,2},{7,3},{8,12},{9,13},{10,... | collective-permute-start | bytes 1572872 | tf_op jit(solution)/shard_map/ppermute | solution.py:167
  520.0 47.7 %all-to-all-start.3 = ((bf16[4,512,768]{1,2,0:T(8,128)(2,1)}), bf16[4,512,768]{1,2,0:T(8,128)(2,1)S(1)}, u32[]{:S(2)}, u32[]{:S(2)}) async-start(bf16[4,512,768]{1,2,0:T(8,128)(2,1)} %copy.110), calls=%async_computation.3 | async-start | bytes 6291456 | tf_op jit(solution)/shard_map/all_to_all | solution.py:261
  536.1 30.1 %copy-start.20 = (f32[32,4096]{1,0:T(8,128)S(1)}, f32[32,4096]{1,0:T(8,128)}, u32[]{:S(2)}) copy-start(f32[32,4096]{1,0:T(8,128)} %param.25) | copy-start | bytes 1572868
  536.1 30.1 %copy-start.28 = (f32[32,4096]{1,0:T(8,128)S(1)}, f32[32,4096]{1,0:T(8,128)}, u32[]{:S(2)}) copy-start(f32[32,4096]{1,0:T(8,128)} %param.27) | copy-start | bytes 1572868
  536.1 30.1 %copy-start.29 = (f32[32,4096]{1,0:T(8,128)S(1)}, f32[32,4096]{1,0:T(8,128)}, u32[]{:S(2)}) copy-start(f32[32,4096]{1,0:T(8,128)} %param.26) | copy-start | bytes 1572868
  536.1 14.5 %collective-permute-start.28 = (bf16[2,128,1024]{2,1,0:T(8,128)(2,1)S(1)}, bf16[2,128,1024]{2,1,0:T(8,128)(2,1)S(1)}, u32[]{:S(2)}, u32[]{:S(2)}) collective-permute-start(bf16[2,128,1024]{2,1,0:T(8,128)(2,1)S(1)} %dynamic-slice_bitcast_fusion.7), channel_id=1, source_target_pairs={{0,2},{1,3},{2,0},{3,1},{4,6},{5,7},{6,4},{7,5},{8,10},{9,11},{10,... | collective-permute-start | bytes 1572872 | tf_op jit(solution)/shard_map/ppermute | solution.py:167
  540.8 25.4 %collective-permute-start.26 = (bf16[32,4096]{1,0:T(8,128)(2,1)S(1)}, bf16[32,4096]{1,0:T(8,128)(2,1)S(1)}, u32[]{:S(2)}, u32[]{:S(2)}) collective-permute-start(bf16[32,4096]{1,0:T(8,128)(2,1)S(1)} %dynamic-slice_bitcast_fusion.13), channel_id=1, source_target_pairs={{0,16},{8,24},{16,0},{24,8},{1,17},{9,25},{17,1},{25,9},{2,18},{10... | collective-permute-start | bytes 786440 | tf_op jit(solution)/shard_map/ppermute | solution.py:167
  551.6 28.1 %collective-permute-start.29 = (bf16[128,1024]{1,0:T(8,128)(2,1)}, bf16[128,1024]{1,0:T(8,128)(2,1)}, u32[]{:S(2)}, u32[]{:S(2)}) collective-permute-start(bf16[128,1024]{1,0:T(8,128)(2,1)} %dynamic-slice_bitcast_fusion.12), channel_id=1, source_target_pairs={{0,4},{1,5},{2,6},{3,7},{4,0},{5,1},{6,2},{7,3},{8,12},{9,13},{10,... | collective-permute-start | bytes 786440 | tf_op jit(solution)/shard_map/ppermute | solution.py:167
  579.6 3.1 collective-permute-start.30
  582.7 11.3 %collective-permute-start.31 = (f32[2,2,2,1,384]{4,2,1,0,3:T(2,128)S(1)}, f32[2,2,2,1,384]{4,2,1,0,3:T(2,128)S(1)}, u32[]{:S(2)}, u32[]{:S(2)}) collective-permute-start(f32[2,2,2,1,384]{4,2,1,0,3:T(2,128)S(1)} %fusion.45), channel_id=1, source_target_pairs={{0,16},{8,24},{16,0},{24,8},{1,17},{9,25},{17,1},{25,9},{2,18},{10... | collective-permute-start | bytes 36872 | tf_op jit(solution)/shard_map/ppermute | solution.py:167
  594.1 10.4 %collective-permute-start.32 = (f32[2,2,1,384]{3,2,1,0:T(1,128)S(1)}, f32[2,2,1,384]{3,2,1,0:T(1,128)S(1)}, u32[]{:S(2)}, u32[]{:S(2)}) collective-permute-start(f32[2,2,1,384]{3,2,1,0:T(1,128)S(1)} %fusion.49), channel_id=1, source_target_pairs={{0,1},{1,0},{2,3},{3,2},{4,5},{5,4},{6,7},{7,6},{8,9},{9,8},{10,11... | collective-permute-start | bytes 18440 | tf_op jit(solution)/shard_map/ppermute | solution.py:167
  599.6 18.4 %collective-permute-start.15 = (bf16[2,2,2,2,32,1536]{5,4,0,1,2,3:T(8,128)(2,1)}, bf16[2,2,2,2,32,1536]{5,4,0,1,2,3:T(8,128)(2,1)}, u32[]{:S(2)}, u32[]{:S(2)}) collective-permute-start(bf16[2,2,2,2,32,1536]{5,4,0,1,2,3:T(8,128)(2,1)} %bitcast.264), channel_id=1, source_target_pairs={{0,8},{8,0},{16,24},{24,16},{1,9},{9,1},{17,25},{25,17},{2,10},{10... | collective-permute-start | bytes 4718600 | tf_op jit(solution)/shard_map/ppermute | solution.py:167
  604.5 4.6 collective-permute-start.33
  608.8 12.9 %collective-permute-start.10 = (bf16[2,2,2,2,32,1536]{5,4,3,2,1,0:T(8,128)(2,1)}, bf16[2,2,2,2,32,1536]{5,4,3,2,1,0:T(8,128)(2,1)}, u32[]{:S(2)}, u32[]{:S(2)}) collective-permute-start(bf16[2,2,2,2,32,1536]{5,4,3,2,1,0:T(8,128)(2,1)} %dynamic-slice_bitcast_fusion.2), channel_id=1, source_target_pairs={{0,8},{8,0},{16,24},{24,16},{1,9},{9,1},{17,25},{25,17},{2,10},{10... | collective-permute-start | bytes 4718600 | tf_op jit(solution)/shard_map/ppermute | solution.py:167
  609.1 8.8 %collective-permute-start.34 = (f32[1,384]{1,0:T(1,128)S(1)}, f32[1,384]{1,0:T(1,128)S(1)}, u32[]{:S(2)}, u32[]{:S(2)}) collective-permute-start(f32[1,384]{1,0:T(1,128)S(1)} %fusion.56), channel_id=1, source_target_pairs={{0,4},{1,5},{2,6},{3,7},{4,0},{5,1},{6,2},{7,3},{8,12},{9,13},{10,... | collective-permute-start | bytes 4616 | tf_op jit(solution)/shard_map/ppermute | solution.py:167
  620.6 19.3 %collective-permute-start.16 = (bf16[2,2,2,32,1536]{4,3,0,1,2:T(8,128)(2,1)S(1)}, bf16[2,2,2,32,1536]{4,3,0,1,2:T(8,128)(2,1)S(1)}, u32[]{:S(2)}, u32[]{:S(2)}) collective-permute-start(bf16[2,2,2,32,1536]{4,3,0,1,2:T(8,128)(2,1)S(1)} %dynamic-slice_bitcast_fusion.5), channel_id=1, source_target_pairs={{0,1},{1,0},{2,3},{3,2},{4,5},{5,4},{6,7},{7,6},{8,9},{9,8},{10,11... | collective-permute-start | bytes 2359304 | tf_op jit(solution)/shard_map/ppermute | solution.py:167
  623.7 19.0 %collective-permute-start.11 = (bf16[2,2,2,32,1536]{4,3,2,1,0:T(8,128)(2,1)S(1)}, bf16[2,2,2,32,1536]{4,3,2,1,0:T(8,128)(2,1)S(1)}, u32[]{:S(2)}, u32[]{:S(2)}) collective-permute-start(bf16[2,2,2,32,1536]{4,3,2,1,0:T(8,128)(2,1)S(1)} %dynamic-slice_bitcast_fusion.6), channel_id=1, source_target_pairs={{0,16},{8,24},{16,0},{24,8},{1,17},{9,25},{17,1},{25,9},{2,18},{10... | collective-permute-start | bytes 2359304 | tf_op jit(solution)/shard_map/ppermute | solution.py:167
  640.2 10.0 %collective-permute-start.17 = (bf16[2,2,32,1536]{3,2,0,1:T(8,128)(2,1)S(1)}, bf16[2,2,32,1536]{3,2,0,1:T(8,128)(2,1)S(1)}, u32[]{:S(2)}, u32[]{:S(2)}) collective-permute-start(bf16[2,2,32,1536]{3,2,0,1:T(8,128)(2,1)S(1)} %dynamic-slice_bitcast_fusion.10), channel_id=1, source_target_pairs={{0,2},{1,3},{2,0},{3,1},{4,6},{5,7},{6,4},{7,5},{8,10},{9,11},{10,... | collective-permute-start | bytes 1179656 | tf_op jit(solution)/shard_map/ppermute | solution.py:167
  643.0 9.7 %collective-permute-start.12 = (bf16[2,2,32,1536]{3,2,1,0:T(8,128)(2,1)S(1)}, bf16[2,2,32,1536]{3,2,1,0:T(8,128)(2,1)S(1)}, u32[]{:S(2)}, u32[]{:S(2)}) collective-permute-start(bf16[2,2,32,1536]{3,2,1,0:T(8,128)(2,1)S(1)} %dynamic-slice_bitcast_fusion.11), channel_id=1, source_target_pairs={{0,1},{1,0},{2,3},{3,2},{4,5},{5,4},{6,7},{7,6},{8,9},{9,8},{10,11... | collective-permute-start | bytes 1179656 | tf_op jit(solution)/shard_map/ppermute | solution.py:167
  650.4 10.1 %collective-permute-start.18 = (bf16[2,32,1536]{2,1,0:T(8,128)(2,1)S(1)}, bf16[2,32,1536]{2,1,0:T(8,128)(2,1)S(1)}, u32[]{:S(2)}, u32[]{:S(2)}) collective-permute-start(bf16[2,32,1536]{2,1,0:T(8,128)(2,1)S(1)} %dynamic-slice_bitcast_fusion.15), channel_id=1, source_target_pairs={{0,4},{1,5},{2,6},{3,7},{4,0},{5,1},{6,2},{7,3},{8,12},{9,13},{10,... | collective-permute-start | bytes 589832 | tf_op jit(solution)/shard_map/ppermute | solution.py:167
  652.9 9.4 %collective-permute-start.13 = (bf16[2,32,1536]{2,1,0:T(8,128)(2,1)S(1)}, bf16[2,32,1536]{2,1,0:T(8,128)(2,1)S(1)}, u32[]{:S(2)}, u32[]{:S(2)}) collective-permute-start(bf16[2,32,1536]{2,1,0:T(8,128)(2,1)S(1)} %dynamic-slice_bitcast_fusion.16), channel_id=1, source_target_pairs={{0,2},{1,3},{2,0},{3,1},{4,6},{5,7},{6,4},{7,5},{8,10},{9,11},{10,... | collective-permute-start | bytes 589832 | tf_op jit(solution)/shard_map/ppermute | solution.py:167
  660.5 4.7 collective-permute-start.19
  662.3 5.9 collective-permute-start.14
  (36 other events, 231.5 us)
Sparse Core Ops, SparseCore 0:
  11.5 72.2 all-gather.4
  87.4 59.0 all-gather.6
  150.0 77.8 all-gather.8
  231.3 78.0 all-gather.10
